TPU v7x, 256 devices: a whole 4x4x8 slice. The times are simulated.
256 devices in a mesh: band: 32 (over z, x), gvec: 8 (over y, core).
Axes of the slice: x: 4, y: 4, z: 8, core: 2. Of those that a mesh axis runs over, the one named last changes fastest.
Arguments:
- pairs: bfloat16 [32, 8, 512, 640], P(None, 'gvec', 'band'), may hold values from -0.59765625 to 0.59765625
- cond_energy: float32 [512], replicated, may hold values from 0.5 to 12
- val_energy: float32 [32, 8], replicated, may hold values from -12 to -2
- band_counts: int32 [32], replicated, may hold values from 1 to 16, as said below
- slab: int32 [1], replicated, may hold values from 0 to 31
Outputs:
- chi_zero: float32 [20480, 20480], P('gvec', 'band')
Inputs may be any that keep to these rules, and one draw needn't show every extreme that they name: `band_counts`: every owner has at least one occupied slot, and in every draw some owner has all 16 slots occupied.
All inputs are finite; a program needn't handle non-finite values.
Results may differ from a plain program's by a relative error of at most 0.0028.
Values may be sent and summed in bfloat16 or wider, within the bound.
No kernel may reach another device: no remote copies, remote signals or barrier semaphores. Data moves between devices by JAX's collectives and lax.ppermute only.
A program may use at most 128 MiB of HBM per device.

v0:
```python
import jax
import jax.numpy as jnp
from jax import lax
from jax.sharding import PartitionSpec as P


def on_device(pairs, cond_energy, val_energy, band_counts, slab):
    n_band = lax.axis_size("band")
    n_gvec = lax.axis_size("gvec")
    ratio = n_band // n_gvec
    local_v = pairs.shape[1]
    slot_count = pairs.shape[2]
    col_width = pairs.shape[3]
    energies = lax.dynamic_index_in_dim(val_energy, slab[0], 0, keepdims=False)
    slots = jnp.arange(slot_count, dtype=jnp.int32)
    live = (slots[None, :] < band_counts[:, None]).reshape(-1)
    weight = jnp.where(
        live[None, :], 2.0 / (energies[:, None] - cond_energy[None, :]), jnp.float32(0.0)
    )
    blocked = pairs.reshape(n_gvec, ratio, local_v, slot_count, col_width)
    by_block = lax.all_to_all(blocked, "gvec", split_axis=0, concat_axis=2, tiled=True)
    rows_all = lax.all_gather(by_block, "band", axis=3, tiled=True)[0]
    by_column = lax.all_to_all(pairs, "band", split_axis=0, concat_axis=2, tiled=True)
    cols_all = lax.all_gather(by_column, "gvec", axis=1, tiled=True)[0]
    scaled = (weight[:, :, None] * cols_all.astype(jnp.float32)).astype(jnp.bfloat16)
    result = lax.dot_general(
        rows_all, scaled, (((1, 2), (0, 1)), ((), ())), preferred_element_type=jnp.float32
    )
    return result.reshape(ratio * col_width, col_width)


def solution(mesh):
    in_specs = (P(None, "gvec", "band", None), P(), P(), P(), P())
    out_specs = P("gvec", "band")
    return jax.shard_map(
        on_device, mesh=mesh, in_specs=in_specs, out_specs=out_specs, check_vma=False
    )
```

profile of v0, /device:TPU:1, one launch (start us, length us, event | category | flops | bytes accessed | tf_op | source)
XLA Modules:
  0.0 263.4 jit_solution(6837848196494836438)
XLA Ops:
  6.5 0.0 copy-start
  6.5 0.0 all-gather.6.cloned.1.call-start
  6.5 17.7 %all_to_all.30 = bf16[8,4,1,16,640]{4,3,2,1,0:T(8,128)(2,1)S(1)} all-to-all(bf16[8,4,1,16,640]{4,3,2,1,0:T(8,128)(2,1)} %bitcast.24), channel_id=1, replica_groups=mesh['band'=32,'gvec'=8] {'gvec'}, dimensions={0} | all-to-all | bytes 1310720 | tf_op jit(solution)/shard_map/all_to_all | solution.py:21
  24.3 1.2 copy.8
  25.5 0.0 all-gather.6.cloned.1.call-update
  25.5 0.0 all-gather.4.cloned.1.call-start
  25.6 32.6 %all_to_all.31 = bf16[32,1,16,640]{3,2,1,0:T(8,128)(2,1)} all-to-all(bf16[32,1,16,640]{3,2,1,0:T(8,128)(2,1)} %param.5), channel_id=1, replica_groups=mesh['band'=32,'gvec'=8] {'band'}, dimensions={0} | all-to-all | bytes 1310720 | tf_op jit(solution)/shard_map/all_to_all | solution.py:23
  58.2 0.0 all-gather.4.cloned.1.call-update
  58.8 0.7 iota_compare_fusion
  59.6 0.1 lt.27
  59.7 0.0 copy-done
  59.7 0.2 dynamic-slice_reduce_fusion
  59.8 0.8 divide_select_fusion
  60.6 133.8 %all-gather.6.cloned.1.call-done = bf16[1,4,8,1,512,640]{5,2,3,1,0,4:T(8,128)(2,1)} async-done(((bf16[1,4,8,1,16,640]{5,2,3,1,0,4:T(8,128)(2,1)}), bf16[1,4,8,1,512,640]{5,2,3,1,0,4:T(8,128)(2,1)}) %all-gather.6.cloned.1.call-update) | async-done | bytes 20971536 | tf_op jit(solution)/shard_map/all_gather | solution.py:22
  194.4 30.2 %copy.9 = bf16[1,4,8,1,512,640]{4,5,2,1,3,0:T(8,128)(2,1)} copy(bf16[1,4,8,1,512,640]{5,2,3,1,0,4:T(8,128)(2,1)} %all-gather.6.cloned.1.call-done) | data formatting | bytes 41943040 | tf_op jit(solution)/shard_map/all_gather | solution.py:22
  224.6 8.6 %all-gather.4.cloned.1.call-done = bf16[1,8,512,640]{3,2,0,1:T(8,128)(2,1)} async-done(((bf16[1,1,512,640]{3,2,0,1:T(8,128)(2,1)}), bf16[1,8,512,640]{3,2,0,1:T(8,128)(2,1)}) %all-gather.4.cloned.1.call-update) | async-done | bytes 5242896 | tf_op jit(solution)/shard_map/all_gather | solution.py:24
  233.3 23.3 %fusion = f32[640,4,640,1]{0,2,3,1:T(8,128)} fusion(bf16[1,4,8,1,512,640]{4,5,2,1,3,0:T(8,128)(2,1)} %copy.9, bf16[1,8,512,640]{3,2,0,1:T(8,128)(2,1)} %all-gather.4.cloned.1.call-done, f32[8,512]{1,0:T(8,128)S(1)} %divide_select_fusion), kind=kOutput, calls=%fused_computation | convolution fusion | flops 13429637120 | bytes 32784384 | tf_op jit(solution)/shard_map/dot_general | solution.py:26
Async XLA Ops:
  6.5 53.1 %copy-start = (f32[32,8]{0,1:T(8,128)S(1)}, f32[32,8]{0,1:T(8,128)}, u32[]{:S(2)}) copy-start(f32[32,8]{0,1:T(8,128)} %param.7) | copy-start | bytes 3076
  6.5 187.9 %all-gather.6.cloned.1.call-start = ((), (), s32[]{:S(2)}) async-start(), calls=%async_computation.3 | async-start | bytes 21626880 | tf_op jit(solution)/shard_map/all_gather | solution.py:22
  25.5 207.7 %all-gather.4.cloned.1.call-start = ((), (), s32[]{:S(2)}) async-start(), calls=%async_computation.2 | async-start | bytes 5898240 | tf_op jit(solution)/shard_map/all_gather | solution.py:24
Sparse Core Ops, SparseCore 0:
  25.6 168.7 all-gather.5
  196.3 36.9 all-gather.3
where the time goes:
time: 264 us; the launch traced here: 263 us
  waiting for transfers between devices  142 us (54%)
  blocking collectives  50.3 us (19%)
  local copies, waits for them, and re-layouts  31.7 us (12%)
  matrix products  23.3 us (9%)
  between operations  14.1 us (5%)
    all_gather x1, waiting for transfers between devices, on_device(): rows_all = lax.all_gather(by_block, 'band', axis=3, tiled=True)[0]  134 us
    all_to_all x1, blocking collectives, on_device(): lax.all_to_all(pairs, 'band', split_axis=0, concat_axis=2, tiled=True)  32.6 us
    all_gather x1, local copies, waits for them, and re-layouts, on_device(): rows_all = lax.all_gather(by_block, 'band', axis=3, tiled=True)[0]  30.2 us
    dot_general x1, matrix products, on_device(): lax.dot_general(rows_all, scaled, (((1, 2), (0, 1)), ((), ())), preferred...  23.3 us
    all_to_all x1, blocking collectives, on_device(): lax.all_to_all(blocked, 'gvec', split_axis=0, concat_axis=2, tiled=True)  17.7 us
    all_gather x1, waiting for transfers between devices, on_device(): cols_all = lax.all_gather(by_column, 'gvec', axis=1, tiled=True)[0]  8.62 us
  transfers between devices with their start and end apart: 2, of which 2 were waited for; matrix products, arithmetic and copies ran while one was open for 12% of the time, Pallas kernels for 0%

commit v1 on v0

--- a/solution.py
+++ b/solution.py
@@ -21,7 +21,9 @@
     by_block = lax.all_to_all(blocked, "gvec", split_axis=0, concat_axis=2, tiled=True)
     rows_all = lax.all_gather(by_block, "band", axis=3, tiled=True)[0]
     by_column = lax.all_to_all(pairs, "band", split_axis=0, concat_axis=2, tiled=True)
-    cols_all = lax.all_gather(by_column, "gvec", axis=1, tiled=True)[0]
+    cols_all = jnp.concatenate(
+        lax.all_to_all(jnp.stack([by_column] * lax.axis_size("gvec")), "gvec", 0, 0), axis=1
+    )[0]
     scaled = (weight[:, :, None] * cols_all.astype(jnp.float32)).astype(jnp.bfloat16)
     result = lax.dot_general(
         rows_all, scaled, (((1, 2), (0, 1)), ((), ())), preferred_element_type=jnp.float32

time: 264 us -> 256 us (0.970)
  waiting for transfers between devices: 142 us -> 124 us
  starting transfers between devices: 0.04 us -> 8.68 us
    all_gather x1, waiting for transfers between devices: 134 us -> 124 us  [on_device(): rows_all = lax.all_gather(by_block, 'band', axis=3, tiled=True)[0]]
    all_to_all x0 -> x1, starting transfers between devices: none -> 8.68 us  [on_device(): lax.all_to_all(jnp.stack([by_column] * lax.axis_size('gvec')), 'gvec', 0, 0)]
    all_gather x1 -> x0, waiting for transfers between devices: 8.62 us -> none  [on_device(): cols_all = lax.all_gather(by_column, 'gvec', axis=1, tiled=True)[0]]
    another operation x0 -> x1, local copies, waits for them, and re-layouts: none -> 2.78 us  [on_device(): jnp.stack([by_column] * lax.axis_size('gvec'))]
  transfers between devices with their start and end apart: 2 -> 2, of which waited for: 2 -> 1; matrix products, arithmetic and copies ran while one was open for 12% -> 13% of each run, Pallas kernels for 0% -> 0%
where the time goes in v1:
time: 256 us; the launch traced here: 255 us
  waiting for transfers between devices  124 us (48%)
  blocking collectives  50.3 us (20%)
  local copies, waits for them, and re-layouts  34.3 us (13%)
  matrix products  23.3 us (9%)
  between operations  14.1 us (6%)
  starting transfers between devices  8.68 us (3%)
    all_gather x1, waiting for transfers between devices, on_device(): rows_all = lax.all_gather(by_block, 'band', axis=3, tiled=True)[0]  124 us
    all_to_all x1, blocking collectives, on_device(): lax.all_to_all(pairs, 'band', split_axis=0, concat_axis=2, tiled=True)  32.5 us
    all_gather x1, local copies, waits for them, and re-layouts, on_device(): rows_all = lax.all_gather(by_block, 'band', axis=3, tiled=True)[0]  30.1 us
    dot_general x1, matrix products, on_device(): lax.dot_general(rows_all, scaled, (((1, 2), (0, 1)), ((), ())), preferred...  23.3 us
    all_to_all x1, blocking collectives, on_device(): lax.all_to_all(blocked, 'gvec', split_axis=0, concat_axis=2, tiled=True)  17.8 us
    all_to_all x1, starting transfers between devices, on_device(): lax.all_to_all(jnp.stack([by_column] * lax.axis_size('gvec')), 'gvec', 0, 0)  8.68 us
  transfers between devices with their start and end apart: 2, of which 1 were waited for; matrix products, arithmetic and copies ran while one was open for 13% of the time, Pallas kernels for 0%

profile of v1, /device:TPU:1, one launch (start us, length us, event | category | flops | bytes accessed | tf_op | source)
XLA Modules:
  0.0 254.7 jit_solution(16022949856824807583)
XLA Ops:
  6.5 0.0 copy-start
  6.5 0.0 all-gather.3.cloned.1.call-start
  6.5 0.0 copy-start.2
  6.5 0.0 copy-start.1
  6.5 17.8 %all_to_all.32 = bf16[8,4,1,16,640]{4,3,2,1,0:T(8,128)(2,1)S(1)} all-to-all(bf16[8,4,1,16,640]{4,3,2,1,0:T(8,128)(2,1)} %bitcast.25), channel_id=1, replica_groups=mesh['band'=32,'gvec'=8] {'gvec'}, dimensions={0} | all-to-all | bytes 1310720 | tf_op jit(solution)/shard_map/all_to_all | solution.py:21
  24.3 1.2 copy.8
  25.5 0.0 all-gather.3.cloned.1.call-update
  25.5 32.5 %all_to_all.33 = bf16[32,1,16,640]{3,2,1,0:T(8,128)(2,1)S(1)} all-to-all(bf16[32,1,16,640]{3,2,1,0:T(8,128)(2,1)} %param.5), channel_id=1, replica_groups=mesh['band'=32,'gvec'=8] {'band'}, dimensions={0} | all-to-all | bytes 1310720 | tf_op jit(solution)/shard_map/all_to_all | solution.py:23
  58.1 2.8 %stack.5 = bf16[8,1,1,512,640]{4,3,2,1,0:T(8,128)(2,1)} broadcast(bf16[512,640]{1,0:T(8,128)(2,1)S(1)} %bitcast.27), dimensions={3,4} | broadcast | bytes 5898240 | tf_op jit(solution)/shard_map/stack | solution.py:25
  60.9 8.7 %all-to-all-start.1 = ((bf16[8,1,1,512,640]{4,3,2,1,0:T(8,128)(2,1)}), bf16[8,1,1,512,640]{4,3,2,1,0:T(8,128)(2,1)}, u32[]{:S(2)}, u32[]{:S(2)}) async-start(bf16[8,1,1,512,640]{4,3,2,1,0:T(8,128)(2,1)} %stack.5), calls=%async_computation.1 | async-start | bytes 10485760 | tf_op jit(solution)/shard_map/all_to_all | solution.py:25
  70.2 0.0 copy-done.2
  70.2 0.1 iota_compare_fusion
  70.3 0.1 lt.27
  70.4 0.0 copy-done
  70.4 0.2 dynamic-slice_reduce_fusion
  70.6 0.0 copy-done.1
  70.6 0.1 divide_select_fusion
  70.6 123.8 %all-gather.3.cloned.1.call-done = bf16[1,4,8,1,512,640]{5,2,3,1,0,4:T(8,128)(2,1)} async-done(((bf16[1,4,8,1,16,640]{5,2,3,1,0,4:T(8,128)(2,1)}), bf16[1,4,8,1,512,640]{5,2,3,1,0,4:T(8,128)(2,1)}) %all-gather.3.cloned.1.call-update) | async-done | bytes 20971536 | tf_op jit(solution)/shard_map/all_gather | solution.py:22
  194.5 30.1 %copy.9 = bf16[1,4,8,1,512,640]{4,5,2,1,3,0:T(8,128)(2,1)} copy(bf16[1,4,8,1,512,640]{5,2,3,1,0,4:T(8,128)(2,1)} %all-gather.3.cloned.1.call-done) | data formatting | bytes 41943040 | tf_op jit(solution)/shard_map/all_gather | solution.py:22
  224.5 0.0 all-to-all-done.1
  224.5 23.3 %fusion = f32[640,4,640,1]{0,2,3,1:T(8,128)} fusion(bf16[1,4,8,1,512,640]{4,5,2,1,3,0:T(8,128)(2,1)} %copy.9, bf16[8,1,1,512,640]{4,3,2,1,0:T(8,128)(2,1)} %all-to-all-done.1, f32[8,512]{1,0:T(8,128)S(1)} %divide_select_fusion), kind=kOutput, calls=%fused_computation | convolution fusion | flops 13429637120 | bytes 32784384 | tf_op jit(solution)/shard_map/dot_general | solution.py:28
Async XLA Ops:
  6.5 63.8 %copy-start = (f32[32,8]{0,1:T(8,128)S(1)}, f32[32,8]{0,1:T(8,128)}, u32[]{:S(2)}) copy-start(f32[32,8]{0,1:T(8,128)} %param.7) | copy-start | bytes 3076
  6.5 187.9 %all-gather.3.cloned.1.call-start = ((), (), s32[]{:S(2)}) async-start(), calls=%async_computation.3 | async-start | bytes 21626880 | tf_op jit(solution)/shard_map/all_gather | solution.py:22
  6.5 63.7 %copy-start.2 = (s32[32]{0:T(128)S(1)}, s32[32]{0:T(128)}, u32[]{:S(2)}) copy-start(s32[32]{0:T(128)} %param.8) | copy-start | bytes 388
  6.5 64.0 %copy-start.1 = (f32[512]{0:T(512)S(1)}, f32[512]{0:T(512)}, u32[]{:S(2)}) copy-start(f32[512]{0:T(512)} %param.6) | copy-start | bytes 6148
  60.9 163.7 %all-to-all-start.1 = ((bf16[8,1,1,512,640]{4,3,2,1,0:T(8,128)(2,1)}), bf16[8,1,1,512,640]{4,3,2,1,0:T(8,128)(2,1)}, u32[]{:S(2)}, u32[]{:S(2)}) async-start(bf16[8,1,1,512,640]{4,3,2,1,0:T(8,128)(2,1)} %stack.5), calls=%async_computation.1 | async-start | bytes 10485760 | tf_op jit(solution)/shard_map/all_to_all | solution.py:25
Sparse Core Ops, SparseCore 0:
  25.7 168.7 all-gather.2
